TPU v7x, 32 devices: a whole 2x2x4 slice. The times are simulated.
32 devices in a mesh: ctx: 4 (over y, core), tp: 4 (over z), rep: 2 (over x).
Axes of the slice: x: 2, y: 2, z: 4, core: 2. Of those that a mesh axis runs over, the one named last changes fastest.
Arguments:
- queries: bfloat16 [1536, 4096], P(('ctx', 'rep'), 'tp'), may hold values from -6 to 6
- key_states: bfloat16 [1536, 1024], P(('ctx', 'rep'), 'tp'), may hold values from -6 to 6
- value_states: bfloat16 [1536, 1024], P(('ctx', 'rep'), 'tp'), may hold values from -6 to 6
- out_grad: bfloat16 [1536, 4096], P(('ctx', 'rep'), 'tp'), may hold values from -6 to 6
- doc_lengths: int32 [7], replicated, may hold values from 0 to 768, as said below
Outputs:
- attended: bfloat16 [1536, 4096], P(('ctx', 'rep'), 'tp')
- query_grad: bfloat16 [1536, 4096], P(('ctx', 'rep'), 'tp')
- key_grad: bfloat16 [1536, 1024], P(('ctx', 'rep'), 'tp')
- value_grad: bfloat16 [1536, 1024], P(('ctx', 'rep'), 'tp')
Inputs may be any that keep to these rules, and one draw needn't show every extreme that they name: `doc_lengths`: the lengths sum to 1536; the largest is exactly 768; some entries are 0.
All inputs are finite; a program needn't handle non-finite values.
Results may differ from a plain program's by a relative error of at most 0.007.
Values may be sent and summed in bfloat16 or wider, within the bound.
A program may use at most 64 MiB of HBM per device.

v0:
```python
import math

import jax
import jax.numpy as jnp
from jax import lax
from jax.sharding import PartitionSpec as P

HD = 128
REACH = 4


masked_score = -1e30


def from_behind(block, axis, distance):
    devices = range(lax.axis_size(axis))
    route = [(i - distance, i) for i in devices if i - distance in devices]
    return lax.ppermute(block, axis, route)


def document_of(doc_ends, positions):
    return jnp.sum((doc_ends[None, :] <= positions[:, None]).astype(jnp.int32), axis=1)


def per_device(queries, key_states, value_states, out_grad, doc_lengths):
    seq_rows = queries.shape[0]
    key_width = key_states.shape[1]
    kv_heads = key_width // HD
    group_size = queries.shape[1] // HD // kv_heads
    scaling = 1.0 / math.sqrt(HD)
    position = lax.axis_index(("ctx", "rep"))
    doc_ends = jnp.cumsum(doc_lengths)
    own_pair = (key_states, value_states)
    received = []
    for distance in range(1, REACH + 1):
        received.append(from_behind((own_pair[0], own_pair[1]), ("ctx", "rep"), distance))
    first_pos = position * seq_rows
    local_pos = first_pos + jnp.arange(seq_rows, dtype=jnp.int32)
    query_doc = document_of(doc_ends, local_pos)

    def allowed_for(key_pos):
        same_doc = document_of(doc_ends, key_pos)[None, :] == query_doc[:, None]
        return same_doc & (key_pos[None, :] <= local_pos[:, None]) & (key_pos[None, :] >= 0)

    block_total = REACH + 1
    key_blocks = [received[REACH - 1 - index][0] for index in range(REACH)] + [key_states]
    value_blocks = [received[REACH - 1 - index][1] for index in range(REACH)] + [value_states]
    block_masks = [
        allowed_for(local_pos - (REACH - index) * seq_rows) for index in range(block_total)
    ]
    attended_cols = []
    query_cols = []
    key_parts = [[] for index in range(block_total)]
    value_parts = [[] for index in range(block_total)]
    for group in range(kv_heads):
        low_col = group * group_size * HD
        high_col = (group + 1) * group_size * HD
        query_group = queries[:, low_col:high_col].reshape(seq_rows, group_size, HD)
        grad_group = out_grad[:, low_col:high_col].reshape(seq_rows, group_size, HD)
        group_keys = [blk[:, group * HD : (group + 1) * HD] for blk in key_blocks]
        group_values = [blk[:, group * HD : (group + 1) * HD] for blk in value_blocks]
        score_blocks = []
        for block_id in range(block_total):

            def score_fn(key_block=group_keys[block_id], block_mask=block_masks[block_id]):
                raw_scores = (
                    jnp.einsum(
                        "tjd,sd->jts", query_group, key_block, preferred_element_type=jnp.float32
                    )
                    * scaling
                )
                return jnp.where(block_mask[None], raw_scores, masked_score)

            score_blocks.append(score_fn())
        row_max = jnp.max(score_blocks[0], axis=-1, keepdims=True)
        for block_id in range(1, block_total):
            row_max = jnp.maximum(row_max, jnp.max(score_blocks[block_id], axis=-1, keepdims=True))
        exp_total = sum(
            (
                jnp.sum(jnp.exp(block_score - row_max), axis=-1, keepdims=True)
                for block_score in score_blocks
            )
        )
        log_total = row_max + jnp.log(exp_total)
        prob_blocks = [jnp.exp(block_score - log_total) for block_score in score_blocks]
        prob_bf_blocks = [block_prob.astype(jnp.bfloat16) for block_prob in prob_blocks]
        attended_acc = jnp.zeros((seq_rows, group_size, HD), jnp.float32)
        for block_id in range(block_total):

            def mix_fn(prob_bf=prob_bf_blocks[block_id], value_block=group_values[block_id]):
                return jnp.einsum(
                    "jts,sd->tjd", prob_bf, value_block, preferred_element_type=jnp.float32
                )

            attended_acc = attended_acc + mix_fn()
        attended_bf = attended_acc.astype(jnp.bfloat16)
        attended_cols.append(attended_bf.reshape(seq_rows, group_size * HD))
        attended_back = lax.optimization_barrier(attended_bf).astype(jnp.float32)
        delta_row = jnp.sum(grad_group.astype(jnp.float32) * attended_back, axis=-1)
        delta_col = jnp.transpose(delta_row)[:, :, None]
        query_acc = jnp.zeros((seq_rows, group_size, HD), jnp.float32)
        for block_id in range(block_total):

            def grad_fn(
                block_prob=prob_blocks[block_id],
                prob_bf=prob_bf_blocks[block_id],
                key_block=group_keys[block_id],
                value_block=group_values[block_id],
            ):
                dprobs = jnp.einsum(
                    "tjd,sd->jts", grad_group, value_block, preferred_element_type=jnp.float32
                )
                dscores = (block_prob * (dprobs - delta_col)).astype(jnp.bfloat16)
                query_term = (
                    jnp.einsum(
                        "jts,sd->tjd", dscores, key_block, preferred_element_type=jnp.float32
                    )
                    * scaling
                )
                key_term = (
                    jnp.einsum(
                        "jts,tjd->sd", dscores, query_group, preferred_element_type=jnp.float32
                    )
                    * scaling
                )
                value_term = jnp.einsum(
                    "jts,tjd->sd", prob_bf, grad_group, preferred_element_type=jnp.float32
                )
                return (query_term, key_term, value_term)

            query_term, key_term, value_term = grad_fn()
            query_acc = query_acc + query_term
            key_parts[block_id].append(key_term)
            value_parts[block_id].append(value_term)
        query_cols.append(query_acc.astype(jnp.bfloat16).reshape(seq_rows, group_size * HD))
    attended = jnp.concatenate(attended_cols, axis=1)
    query_grad = jnp.concatenate(query_cols, axis=1)
    key_cat = [jnp.concatenate(key_parts[index], axis=1) for index in range(block_total)]
    value_cat = [jnp.concatenate(value_parts[index], axis=1) for index in range(block_total)]
    key_total = key_cat[REACH]
    value_total = value_cat[REACH]
    for step in range(REACH):
        arrived = (
            from_behind(key_cat[step].astype(jnp.bfloat16), ("ctx", "rep"), step - REACH).astype(
                jnp.float32
            ),
            from_behind(value_cat[step].astype(jnp.bfloat16), ("ctx", "rep"), step - REACH).astype(
                jnp.float32
            ),
        )
        key_total = key_total + arrived[0]
        value_total = value_total + arrived[1]
    return (attended, query_grad, key_total.astype(jnp.bfloat16), value_total.astype(jnp.bfloat16))


def solution(mesh):
    in_specs = (
        P(("ctx", "rep"), "tp"),
        P(("ctx", "rep"), "tp"),
        P(("ctx", "rep"), "tp"),
        P(("ctx", "rep"), "tp"),
        P(),
    )
    out_specs = (
        P(("ctx", "rep"), "tp"),
        P(("ctx", "rep"), "tp"),
        P(("ctx", "rep"), "tp"),
        P(("ctx", "rep"), "tp"),
    )
    return jax.shard_map(
        per_device, mesh=mesh, in_specs=in_specs, out_specs=out_specs, check_vma=False
    )
```

profile of v0, /device:TPU:0, one launch (start us, length us, event | category | flops | bytes accessed | tf_op | source)
XLA Modules:
  0.0 69.6 jit_solution(11482073747919994690)
XLA Ops:
  0.6 4.8 %collective-permute-start.3 = (bf16[192,256]{1,0:T(8,128)(2,1)}, bf16[192,256]{1,0:T(8,128)(2,1)S(1)}, u32[]{:S(2)}, u32[]{:S(2)}) collective-permute-start(bf16[192,256]{1,0:T(8,128)(2,1)} %param.6), channel_id=1, source_target_pairs={{0,1},{1,8},{8,9},{9,16},{16,17},{17,24},{24,25},{2,3},{3,10},{10,... | collective-permute-start | bytes 294920 | tf_op jit(solution)/shard_map/ppermute | solution.py:18
  5.5 1.5 %collective-permute-start.2 = (bf16[192,256]{1,0:T(8,128)(2,1)}, bf16[192,256]{1,0:T(8,128)(2,1)S(1)}, u32[]{:S(2)}, u32[]{:S(2)}) collective-permute-start(bf16[192,256]{1,0:T(8,128)(2,1)} %param.6), channel_id=1, source_target_pairs={{0,8},{1,9},{8,16},{9,17},{16,24},{17,25},{2,10},{3,11},{10,18},{1... | collective-permute-start | bytes 294920 | tf_op jit(solution)/shard_map/ppermute | solution.py:18
  7.0 3.6 %collective-permute-start.1 = (bf16[192,256]{1,0:T(8,128)(2,1)}, bf16[192,256]{1,0:T(8,128)(2,1)S(1)}, u32[]{:S(2)}, u32[]{:S(2)}) collective-permute-start(bf16[192,256]{1,0:T(8,128)(2,1)} %param.6), channel_id=1, source_target_pairs={{0,9},{1,16},{8,17},{9,24},{16,25},{2,11},{3,18},{10,19},{11,26},{... | collective-permute-start | bytes 294920 | tf_op jit(solution)/shard_map/ppermute | solution.py:18
  10.6 2.2 %collective-permute-start = (bf16[192,256]{1,0:T(8,128)(2,1)}, bf16[192,256]{1,0:T(8,128)(2,1)S(1)}, u32[]{:S(2)}, u32[]{:S(2)}) collective-permute-start(bf16[192,256]{1,0:T(8,128)(2,1)} %param.6), channel_id=1, source_target_pairs={{0,16},{1,17},{8,24},{9,25},{2,18},{3,19},{10,26},{11,27},{4,20},{... | collective-permute-start | bytes 294920 | tf_op jit(solution)/shard_map/ppermute | solution.py:18
  12.8 2.7 %collective-permute-start.7 = (bf16[192,256]{1,0:T(8,128)(2,1)}, bf16[192,256]{1,0:T(8,128)(2,1)S(1)}, u32[]{:S(2)}, u32[]{:S(2)}) collective-permute-start(bf16[192,256]{1,0:T(8,128)(2,1)} %param.7), channel_id=1, source_target_pairs={{0,1},{1,8},{8,9},{9,16},{16,17},{17,24},{24,25},{2,3},{3,10},{10,... | collective-permute-start | bytes 294920 | tf_op jit(solution)/shard_map/ppermute | solution.py:18
  15.6 1.1 %slice_bitcast_fusion.3 = (bf16[24,4,8,128]{3,2,1,0:T(8,128)(2,1)S(1)}, bf16[24,4,8,128]{3,2,1,0:T(8,128)(2,1)S(1)}) fusion(bf16[192,1024]{1,0:T(8,128)(2,1)} %param.5), kind=kLoop, calls=%fused_computation.231 | loop fusion | bytes 786432
  19.9 0.8 %copy-done = bf16[192,256]{1,0:T(8,128)(2,1)S(1)} copy-done((bf16[192,256]{1,0:T(8,128)(2,1)S(1)}, bf16[192,256]{1,0:T(8,128)(2,1)}, u32[]{:S(2)}) %copy-start) | copy-done | bytes 98328
  20.7 1.3 %collective-permute-start.6 = (bf16[192,256]{1,0:T(8,128)(2,1)S(1)}, bf16[192,256]{1,0:T(8,128)(2,1)S(1)}, u32[]{:S(2)}, u32[]{:S(2)}) collective-permute-start(bf16[192,256]{1,0:T(8,128)(2,1)S(1)} %copy-done), channel_id=1, source_target_pairs={{0,8},{1,9},{8,16},{9,17},{16,24},{17,25},{2,10},{3,11},{10,18},{1... | collective-permute-start | bytes 294920 | tf_op jit(solution)/shard_map/ppermute | solution.py:18
  22.3 2.3 %collective-permute-start.5 = (bf16[192,256]{1,0:T(8,128)(2,1)S(1)}, bf16[192,256]{1,0:T(8,128)(2,1)S(1)}, u32[]{:S(2)}, u32[]{:S(2)}) collective-permute-start(bf16[192,256]{1,0:T(8,128)(2,1)S(1)} %copy-done), channel_id=1, source_target_pairs={{0,9},{1,16},{8,17},{9,24},{16,25},{2,11},{3,18},{10,19},{11,26},{... | collective-permute-start | bytes 294920 | tf_op jit(solution)/shard_map/ppermute | solution.py:18
  24.9 1.3 %collective-permute-start.4 = (bf16[192,256]{1,0:T(8,128)(2,1)S(1)}, bf16[192,256]{1,0:T(8,128)(2,1)S(1)}, u32[]{:S(2)}, u32[]{:S(2)}) collective-permute-start(bf16[192,256]{1,0:T(8,128)(2,1)S(1)} %copy-done), channel_id=1, source_target_pairs={{0,16},{1,17},{8,24},{9,25},{2,18},{3,19},{10,26},{11,27},{4,20},{... | collective-permute-start | bytes 294920 | tf_op jit(solution)/shard_map/ppermute | solution.py:18
  42.1 1.3 %collective-permute-start.15 = (bf16[192,256]{1,0:T(8,128)(2,1)S(1)}, bf16[192,256]{1,0:T(8,128)(2,1)S(1)}, u32[]{:S(2)}, u32[]{:S(2)}) collective-permute-start(bf16[192,256]{1,0:T(8,128)(2,1)S(1)} %pad_maximum_fusion.9), channel_id=1, source_target_pairs={{1,0},{8,1},{9,8},{16,9},{17,16},{24,17},{25,24},{3,2},{10,3},{11,... | collective-permute-start | bytes 294920 | tf_op jit(solution)/shard_map/ppermute | solution.py:18
  43.5 1.3 %collective-permute-start.14 = (bf16[192,256]{1,0:T(8,128)(2,1)S(1)}, bf16[192,256]{1,0:T(8,128)(2,1)S(1)}, u32[]{:S(2)}, u32[]{:S(2)}) collective-permute-start(bf16[192,256]{1,0:T(8,128)(2,1)S(1)} %pad_maximum_fusion.8), channel_id=1, source_target_pairs={{8,0},{9,1},{16,8},{17,9},{24,16},{25,17},{10,2},{11,3},{18,10},{1... | collective-permute-start | bytes 294920 | tf_op jit(solution)/shard_map/ppermute | solution.py:18
  44.8 1.3 %collective-permute-start.13 = (bf16[192,256]{1,0:T(8,128)(2,1)S(1)}, bf16[192,256]{1,0:T(8,128)(2,1)S(1)}, u32[]{:S(2)}, u32[]{:S(2)}) collective-permute-start(bf16[192,256]{1,0:T(8,128)(2,1)S(1)} %pad_maximum_fusion.7), channel_id=1, source_target_pairs={{9,0},{16,1},{17,8},{24,9},{25,16},{11,2},{18,3},{19,10},{26,11},{... | collective-permute-start | bytes 294920 | tf_op jit(solution)/shard_map/ppermute | solution.py:18
  46.1 1.3 %collective-permute-start.12 = (bf16[192,256]{1,0:T(8,128)(2,1)S(1)}, bf16[192,256]{1,0:T(8,128)(2,1)S(1)}, u32[]{:S(2)}, u32[]{:S(2)}) collective-permute-start(bf16[192,256]{1,0:T(8,128)(2,1)S(1)} %pad_maximum_fusion.6), channel_id=1, source_target_pairs={{16,0},{17,1},{24,8},{25,9},{18,2},{19,3},{26,10},{27,11},{20,4},{... | collective-permute-start | bytes 294920 | tf_op jit(solution)/shard_map/ppermute | solution.py:18
  51.1 1.3 %collective-permute-start.9 = (bf16[192,256]{1,0:T(8,128)(2,1)S(1)}, bf16[192,256]{1,0:T(8,128)(2,1)S(1)}, u32[]{:S(2)}, u32[]{:S(2)}) collective-permute-start(bf16[192,256]{1,0:T(8,128)(2,1)S(1)} %pad_maximum_fusion.3), channel_id=1, source_target_pairs={{9,0},{16,1},{17,8},{24,9},{25,16},{11,2},{18,3},{19,10},{26,11},{... | collective-permute-start | bytes 294920 | tf_op jit(solution)/shard_map/ppermute | solution.py:18
  52.5 0.8 %pad_maximum_fusion.1 = bf16[192,1024]{1,0:T(8,128)(2,1)} fusion(bf16[192,512]{1,0:T(8,128)(2,1)S(1)} %bitcast.481, bf16[192,512]{1,0:T(8,128)(2,1)S(1)} %bitcast.480), kind=kLoop, calls=%fused_computation.171 | loop fusion | flops 786432 | bytes 786432 | tf_op jit(solution)/shard_map/concatenate | solution.py:137
  53.2 0.8 %pad_maximum_fusion = bf16[192,1024]{1,0:T(8,128)(2,1)} fusion(bf16[192,512]{1,0:T(8,128)(2,1)S(1)} %copy_bitcast_fusion.2, bf16[192,512]{1,0:T(8,128)(2,1)S(1)} %copy_bitcast_fusion.3), kind=kLoop, calls=%fused_computation.170 | loop fusion | flops 786432 | bytes 786432 | tf_op jit(solution)/shard_map/concatenate | solution.py:136
  54.1 1.3 %collective-permute-start.10 = (bf16[192,256]{1,0:T(8,128)(2,1)S(1)}, bf16[192,256]{1,0:T(8,128)(2,1)S(1)}, u32[]{:S(2)}, u32[]{:S(2)}) collective-permute-start(bf16[192,256]{1,0:T(8,128)(2,1)S(1)} %pad_maximum_fusion.4), channel_id=1, source_target_pairs={{8,0},{9,1},{16,8},{17,9},{24,16},{25,17},{10,2},{11,3},{18,10},{1... | collective-permute-start | bytes 294920 | tf_op jit(solution)/shard_map/ppermute | solution.py:18
  55.4 1.3 %collective-permute-start.11 = (bf16[192,256]{1,0:T(8,128)(2,1)S(1)}, bf16[192,256]{1,0:T(8,128)(2,1)S(1)}, u32[]{:S(2)}, u32[]{:S(2)}) collective-permute-start(bf16[192,256]{1,0:T(8,128)(2,1)S(1)} %pad_maximum_fusion.5), channel_id=1, source_target_pairs={{1,0},{8,1},{9,8},{16,9},{17,16},{24,17},{25,24},{3,2},{10,3},{11,... | collective-permute-start | bytes 294920 | tf_op jit(solution)/shard_map/ppermute | solution.py:18
  56.7 1.3 %collective-permute-start.8 = (bf16[192,256]{1,0:T(8,128)(2,1)S(1)}, bf16[192,256]{1,0:T(8,128)(2,1)S(1)}, u32[]{:S(2)}, u32[]{:S(2)}) collective-permute-start(bf16[192,256]{1,0:T(8,128)(2,1)S(1)} %pad_maximum_fusion.2), channel_id=1, source_target_pairs={{16,0},{17,1},{24,8},{25,9},{18,2},{19,3},{26,10},{27,11},{20,4},{... | collective-permute-start | bytes 294920 | tf_op jit(solution)/shard_map/ppermute | solution.py:18
  58.0 0.7 %fusion.153 = bf16[192,256]{1,0:T(8,128)(2,1)} fusion(f32[192,128]{1,0:T(8,128)S(1)} %convolution_bitcast_fusion.18, f32[192,128]{1,0:T(8,128)S(1)} %convolution_bitcast_fusion.19, bf16[192,256]{1,0:T(8,128)(2,1)S(1)} %collective-permute-done.15, bf16[192,256]{1,0:T(8,128)(2,1)S(1)} %collective-permute-done.14, ...), kind=kLoop, calls=%fused_computation.227 | loop fusion | flops 491520 | bytes 688128 | tf_op jit(solution)/shard_map/convert_element_type | solution.py:153
  59.3 3.2 %collective-permute-done.11 = bf16[192,256]{1,0:T(8,128)(2,1)S(1)} collective-permute-done((bf16[192,256]{1,0:T(8,128)(2,1)S(1)}, bf16[192,256]{1,0:T(8,128)(2,1)S(1)}, u32[]{:S(2)}, u32[]{:S(2)}) %collective-permute-start.11) | collective-permute-done | bytes 98336 | tf_op jit(solution)/shard_map/ppermute | solution.py:18
  62.5 6.4 %collective-permute-done.8 = bf16[192,256]{1,0:T(8,128)(2,1)S(1)} collective-permute-done((bf16[192,256]{1,0:T(8,128)(2,1)S(1)}, bf16[192,256]{1,0:T(8,128)(2,1)S(1)}, u32[]{:S(2)}, u32[]{:S(2)}) %collective-permute-start.8) | collective-permute-done | bytes 98336 | tf_op jit(solution)/shard_map/ppermute | solution.py:18
  68.9 0.7 %fusion.149 = bf16[192,256]{1,0:T(8,128)(2,1)} fusion(f32[192,128]{1,0:T(8,128)S(1)} %fusion.78, f32[192,128]{1,0:T(8,128)S(1)} %fusion.79, bf16[192,256]{1,0:T(8,128)(2,1)S(1)} %collective-permute-done.11, bf16[192,256]{1,0:T(8,128)(2,1)S(1)} %collective-permute-done.10, bf16[192,256]{1,0:T(8,128)(2,1)S(1)} %collective-permute-done.9, ...), kind=kLoop, calls=%fused_computation.222 | loop fusion | flops 491520 | bytes 688128 | tf_op jit(solution)/shard_map/convert_element_type | solution.py:153
  (111 shorter events, 23.7 us)
Async XLA Ops:
  0.6 19.2 %collective-permute-start.3 = (bf16[192,256]{1,0:T(8,128)(2,1)}, bf16[192,256]{1,0:T(8,128)(2,1)S(1)}, u32[]{:S(2)}, u32[]{:S(2)}) collective-permute-start(bf16[192,256]{1,0:T(8,128)(2,1)} %param.6), channel_id=1, source_target_pairs={{0,1},{1,8},{8,9},{9,16},{16,17},{17,24},{24,25},{2,3},{3,10},{10,... | collective-permute-start | bytes 294920 | tf_op jit(solution)/shard_map/ppermute | solution.py:18
  5.5 16.8 %collective-permute-start.2 = (bf16[192,256]{1,0:T(8,128)(2,1)}, bf16[192,256]{1,0:T(8,128)(2,1)S(1)}, u32[]{:S(2)}, u32[]{:S(2)}) collective-permute-start(bf16[192,256]{1,0:T(8,128)(2,1)} %param.6), channel_id=1, source_target_pairs={{0,8},{1,9},{8,16},{9,17},{16,24},{17,25},{2,10},{3,11},{10,18},{1... | collective-permute-start | bytes 294920 | tf_op jit(solution)/shard_map/ppermute | solution.py:18
  7.0 18.0 %collective-permute-start.1 = (bf16[192,256]{1,0:T(8,128)(2,1)}, bf16[192,256]{1,0:T(8,128)(2,1)S(1)}, u32[]{:S(2)}, u32[]{:S(2)}) collective-permute-start(bf16[192,256]{1,0:T(8,128)(2,1)} %param.6), channel_id=1, source_target_pairs={{0,9},{1,16},{8,17},{9,24},{16,25},{2,11},{3,18},{10,19},{11,26},{... | collective-permute-start | bytes 294920 | tf_op jit(solution)/shard_map/ppermute | solution.py:18
  10.6 16.0 %collective-permute-start = (bf16[192,256]{1,0:T(8,128)(2,1)}, bf16[192,256]{1,0:T(8,128)(2,1)S(1)}, u32[]{:S(2)}, u32[]{:S(2)}) collective-permute-start(bf16[192,256]{1,0:T(8,128)(2,1)} %param.6), channel_id=1, source_target_pairs={{0,16},{1,17},{8,24},{9,25},{2,18},{3,19},{10,26},{11,27},{4,20},{... | collective-permute-start | bytes 294920 | tf_op jit(solution)/shard_map/ppermute | solution.py:18
  12.8 17.0 %collective-permute-start.7 = (bf16[192,256]{1,0:T(8,128)(2,1)}, bf16[192,256]{1,0:T(8,128)(2,1)S(1)}, u32[]{:S(2)}, u32[]{:S(2)}) collective-permute-start(bf16[192,256]{1,0:T(8,128)(2,1)} %param.7), channel_id=1, source_target_pairs={{0,1},{1,8},{8,9},{9,16},{16,17},{17,24},{24,25},{2,3},{3,10},{10,... | collective-permute-start | bytes 294920 | tf_op jit(solution)/shard_map/ppermute | solution.py:18
  16.7 0.7 copy-start.3
  17.6 0.9 %copy-start.1 = (bf16[192,256]{1,0:T(8,128)(2,1)S(1)}, bf16[192,256]{1,0:T(8,128)(2,1)}, u32[]{:S(2)}) copy-start(bf16[192,256]{1,0:T(8,128)(2,1)} %param.6) | copy-start | bytes 294916
  18.8 1.0 %copy-start.2 = (bf16[192,1024]{1,0:T(8,128)(2,1)S(1)}, bf16[192,1024]{1,0:T(8,128)(2,1)}, u32[]{:S(2)}) copy-start(bf16[192,1024]{1,0:T(8,128)(2,1)} %param.8) | copy-start | bytes 1179652
  19.8 0.9 %copy-start = (bf16[192,256]{1,0:T(8,128)(2,1)S(1)}, bf16[192,256]{1,0:T(8,128)(2,1)}, u32[]{:S(2)}) copy-start(bf16[192,256]{1,0:T(8,128)(2,1)} %param.7) | copy-start | bytes 294916
  20.7 8.4 %collective-permute-start.6 = (bf16[192,256]{1,0:T(8,128)(2,1)S(1)}, bf16[192,256]{1,0:T(8,128)(2,1)S(1)}, u32[]{:S(2)}, u32[]{:S(2)}) collective-permute-start(bf16[192,256]{1,0:T(8,128)(2,1)S(1)} %copy-done), channel_id=1, source_target_pairs={{0,8},{1,9},{8,16},{9,17},{16,24},{17,25},{2,10},{3,11},{10,18},{1... | collective-permute-start | bytes 294920 | tf_op jit(solution)/shard_map/ppermute | solution.py:18
  22.3 6.1 %collective-permute-start.5 = (bf16[192,256]{1,0:T(8,128)(2,1)S(1)}, bf16[192,256]{1,0:T(8,128)(2,1)S(1)}, u32[]{:S(2)}, u32[]{:S(2)}) collective-permute-start(bf16[192,256]{1,0:T(8,128)(2,1)S(1)} %copy-done), channel_id=1, source_target_pairs={{0,9},{1,16},{8,17},{9,24},{16,25},{2,11},{3,18},{10,19},{11,26},{... | collective-permute-start | bytes 294920 | tf_op jit(solution)/shard_map/ppermute | solution.py:18
  24.9 5.5 %collective-permute-start.4 = (bf16[192,256]{1,0:T(8,128)(2,1)S(1)}, bf16[192,256]{1,0:T(8,128)(2,1)S(1)}, u32[]{:S(2)}, u32[]{:S(2)}) collective-permute-start(bf16[192,256]{1,0:T(8,128)(2,1)S(1)} %copy-done), channel_id=1, source_target_pairs={{0,16},{1,17},{8,24},{9,25},{2,18},{3,19},{10,26},{11,27},{4,20},{... | collective-permute-start | bytes 294920 | tf_op jit(solution)/shard_map/ppermute | solution.py:18
  42.1 11.9 %collective-permute-start.15 = (bf16[192,256]{1,0:T(8,128)(2,1)S(1)}, bf16[192,256]{1,0:T(8,128)(2,1)S(1)}, u32[]{:S(2)}, u32[]{:S(2)}) collective-permute-start(bf16[192,256]{1,0:T(8,128)(2,1)S(1)} %pad_maximum_fusion.9), channel_id=1, source_target_pairs={{1,0},{8,1},{9,8},{16,9},{17,16},{24,17},{25,24},{3,2},{10,3},{11,... | collective-permute-start | bytes 294920 | tf_op jit(solution)/shard_map/ppermute | solution.py:18
  43.5 11.9 %collective-permute-start.14 = (bf16[192,256]{1,0:T(8,128)(2,1)S(1)}, bf16[192,256]{1,0:T(8,128)(2,1)S(1)}, u32[]{:S(2)}, u32[]{:S(2)}) collective-permute-start(bf16[192,256]{1,0:T(8,128)(2,1)S(1)} %pad_maximum_fusion.8), channel_id=1, source_target_pairs={{8,0},{9,1},{16,8},{17,9},{24,16},{25,17},{10,2},{11,3},{18,10},{1... | collective-permute-start | bytes 294920 | tf_op jit(solution)/shard_map/ppermute | solution.py:18
  44.8 11.9 %collective-permute-start.13 = (bf16[192,256]{1,0:T(8,128)(2,1)S(1)}, bf16[192,256]{1,0:T(8,128)(2,1)S(1)}, u32[]{:S(2)}, u32[]{:S(2)}) collective-permute-start(bf16[192,256]{1,0:T(8,128)(2,1)S(1)} %pad_maximum_fusion.7), channel_id=1, source_target_pairs={{9,0},{16,1},{17,8},{24,9},{25,16},{11,2},{18,3},{19,10},{26,11},{... | collective-permute-start | bytes 294920 | tf_op jit(solution)/shard_map/ppermute | solution.py:18
  46.1 11.9 %collective-permute-start.12 = (bf16[192,256]{1,0:T(8,128)(2,1)S(1)}, bf16[192,256]{1,0:T(8,128)(2,1)S(1)}, u32[]{:S(2)}, u32[]{:S(2)}) collective-permute-start(bf16[192,256]{1,0:T(8,128)(2,1)S(1)} %pad_maximum_fusion.6), channel_id=1, source_target_pairs={{16,0},{17,1},{24,8},{25,9},{18,2},{19,3},{26,10},{27,11},{20,4},{... | collective-permute-start | bytes 294920 | tf_op jit(solution)/shard_map/ppermute | solution.py:18
  51.1 8.2 %collective-permute-start.9 = (bf16[192,256]{1,0:T(8,128)(2,1)S(1)}, bf16[192,256]{1,0:T(8,128)(2,1)S(1)}, u32[]{:S(2)}, u32[]{:S(2)}) collective-permute-start(bf16[192,256]{1,0:T(8,128)(2,1)S(1)} %pad_maximum_fusion.3), channel_id=1, source_target_pairs={{9,0},{16,1},{17,8},{24,9},{25,16},{11,2},{18,3},{19,10},{26,11},{... | collective-permute-start | bytes 294920 | tf_op jit(solution)/shard_map/ppermute | solution.py:18
  54.1 5.2 %collective-permute-start.10 = (bf16[192,256]{1,0:T(8,128)(2,1)S(1)}, bf16[192,256]{1,0:T(8,128)(2,1)S(1)}, u32[]{:S(2)}, u32[]{:S(2)}) collective-permute-start(bf16[192,256]{1,0:T(8,128)(2,1)S(1)} %pad_maximum_fusion.4), channel_id=1, source_target_pairs={{8,0},{9,1},{16,8},{17,9},{24,16},{25,17},{10,2},{11,3},{18,10},{1... | collective-permute-start | bytes 294920 | tf_op jit(solution)/shard_map/ppermute | solution.py:18
  55.4 7.1 %collective-permute-start.11 = (bf16[192,256]{1,0:T(8,128)(2,1)S(1)}, bf16[192,256]{1,0:T(8,128)(2,1)S(1)}, u32[]{:S(2)}, u32[]{:S(2)}) collective-permute-start(bf16[192,256]{1,0:T(8,128)(2,1)S(1)} %pad_maximum_fusion.5), channel_id=1, source_target_pairs={{1,0},{8,1},{9,8},{16,9},{17,16},{24,17},{25,24},{3,2},{10,3},{11,... | collective-permute-start | bytes 294920 | tf_op jit(solution)/shard_map/ppermute | solution.py:18
  56.7 12.2 %collective-permute-start.8 = (bf16[192,256]{1,0:T(8,128)(2,1)S(1)}, bf16[192,256]{1,0:T(8,128)(2,1)S(1)}, u32[]{:S(2)}, u32[]{:S(2)}) collective-permute-start(bf16[192,256]{1,0:T(8,128)(2,1)S(1)} %pad_maximum_fusion.2), channel_id=1, source_target_pairs={{16,0},{17,1},{24,8},{25,9},{18,2},{19,3},{26,10},{27,11},{20,4},{... | collective-permute-start | bytes 294920 | tf_op jit(solution)/shard_map/ppermute | solution.py:18
where the time goes:
time: 70.2 us; the launch traced here: 69.6 us
  starting transfers between devices  30 us (43%)
  matrix products  18.5 us (26%)
  waiting for transfers between devices  10.2 us (15%)
  other arithmetic  5.8 us (8%)
  local copies, waits for them, and re-layouts  3.65 us (5%)
  between operations  1.41 us (2%)
    ppermute x16, starting transfers between devices, from_behind(): return lax.ppermute(block, axis, route)  30 us
    ppermute x16, waiting for transfers between devices, from_behind(): return lax.ppermute(block, axis, route)  10.2 us
    unnamed x10, local copies, waits for them, and re-layouts  3.53 us
    dot_general x10, matrix products, grad_fn(): jnp.einsum('jts,sd->tjd', dscores, key_block, preferred_element_type=jnp....  3.35 us
    dot_general x10, matrix products, mix_fn(): jnp.einsum('jts,sd->tjd', prob_bf, value_block, preferred_element_type=jn...  3.33 us
    dot_general x10, matrix products, score_fn(): jnp.einsum('tjd,sd->jts', query_group, key_block, preferred_element_type=...  3.08 us
    dot_general x10, matrix products, grad_fn(): jnp.einsum('jts,tjd->sd', prob_bf, grad_group, preferred_element_type=jnp...  2.97 us
    dot_general x10, matrix products, grad_fn(): jnp.einsum('tjd,sd->jts', grad_group, value_block, preferred_element_type...  2.91 us
  transfers between devices with their start and end apart: 16, of which 3 were waited for; matrix products, arithmetic and copies ran while one was open for 19% of the time, Pallas kernels for 0%

commit v1 on v0

v1 whole, which is shorter than its diff:
```python
import functools
import math

import jax
import jax.numpy as jnp
from jax import lax
from jax.experimental import pallas as pl
from jax.experimental.pallas import tpu as pltpu
from jax.sharding import PartitionSpec as P

HD = 128
REACH = 4
MESH = pl.DeviceIdType.MESH
masked_score = -1e30


def dot(a, b):
    return jnp.dot(a, b, preferred_element_type=jnp.float32)


def kernel(
    n, reps, doc_ref, q_ref, k_ref, v_ref, do_ref, att_ref, dq_ref, dk_ref, dv_ref,
    kv, gout, gin, scores, probs, kv_send, kv_recv, g_send, g_recv,
):
    rows = q_ref.shape[0]
    kv_heads = k_ref.shape[1] // HD
    group_size = q_ref.shape[1] // HD // kv_heads
    width = group_size * rows
    scaling = 1.0 / math.sqrt(HD)
    log2e = math.log2(math.e)
    pos = lax.axis_index("ctx") * reps + lax.axis_index("rep")

    def place(p):
        return {"ctx": p // reps, "rep": lax.rem(p, reps)}

    barrier = pltpu.get_barrier_semaphore()
    for d in range(1, REACH + 1):
        for ok, peer in ((pos + d < n, pos + d), (pos >= d, pos - d)):

            @pl.when(ok)
            def _():
                pl.semaphore_signal(barrier, inc=1, device_id=place(peer), device_id_type=MESH)

    for g in range(kv_heads):
        cols = slice(g * HD, (g + 1) * HD)
        kv[g, 0, :, :HD] = k_ref[:, cols]
        kv[g, 0, :, HD:] = v_ref[:, cols]
    pl.semaphore_wait(barrier, jnp.minimum(pos, REACH) + jnp.minimum(n - 1 - pos, REACH))

    def kv_copy(g, d):
        return pltpu.make_async_remote_copy(
            src_ref=kv.at[g, 0], dst_ref=kv.at[g, d], send_sem=kv_send.at[g, d - 1],
            recv_sem=kv_recv.at[g, d - 1], device_id=place(pos + d), device_id_type=MESH,
        )

    def g_copy(g, d):
        return pltpu.make_async_remote_copy(
            src_ref=gout.at[g, d - 1], dst_ref=gin.at[g, d - 1], send_sem=g_send.at[g, d - 1],
            recv_sem=g_recv.at[g, d - 1], device_id=place(pos - d), device_id_type=MESH,
        )

    for g in range(kv_heads):
        for d in range(1, REACH + 1):

            @pl.when(pos + d < n)
            def _():
                kv_copy(g, d).start()

    for d in range(1, REACH + 1):

        @pl.when(pos < d)
        def _():
            for g in range(kv_heads):
                kv[g, d] = jnp.zeros(kv.shape[2:], kv.dtype)

        @pl.when(pos + d >= n)
        def _():
            for g in range(kv_heads):
                gin[g, d - 1] = jnp.zeros(gin.shape[2:], gin.dtype)

    first = pos * rows
    query_pos = first + lax.rem(lax.broadcasted_iota(jnp.int32, (1, width), 1), rows)
    begin = jnp.zeros((1, width), jnp.int32)
    end = jnp.int32(0)
    for i in range(doc_ref.shape[0]):
        end = end + doc_ref[i]
        begin = jnp.maximum(begin, jnp.where(query_pos >= end, end, 0))

    own_grads = []
    for g in range(kv_heads):
        heads = [g * group_size + j for j in range(group_size)]
        q = jnp.concatenate([q_ref[:, h * HD : (h + 1) * HD] for h in heads], axis=0)
        do = jnp.concatenate([do_ref[:, h * HD : (h + 1) * HD] for h in heads], axis=0)
        q_t = q.T
        do_t = do.T

        top = None
        for d in range(REACH + 1):
            if d:

                @pl.when(pos >= d)
                def _():
                    kv_copy(g, d).wait_recv()

            key_pos = first - d * rows + lax.broadcasted_iota(jnp.int32, (rows, 1), 0)
            allowed = key_pos >= begin
            if d == 0:
                allowed = allowed & (key_pos <= query_pos)
            s = jnp.where(allowed, dot(kv[g, d, :, :HD], q_t) * (scaling * log2e), masked_score)
            scores[d] = s
            most = jnp.max(s, axis=0, keepdims=True)
            top = most if top is None else jnp.maximum(top, most)
        total = jnp.zeros((1, width), jnp.float32)
        for d in range(REACH + 1):
            e = jnp.exp2(scores[d] - top)
            scores[d] = e
            total = total + jnp.sum(e, axis=0, keepdims=True)
        inverse = 1.0 / total
        att_t = jnp.zeros((HD, width), jnp.float32)
        for d in range(REACH + 1):
            p_bf = (scores[d] * inverse).astype(jnp.bfloat16)
            probs[d] = p_bf
            att_t = att_t + dot(kv[g, d, :, HD:].T, p_bf)
        att_bf = att_t.astype(jnp.bfloat16)
        delta = jnp.sum(
            att_bf.astype(jnp.float32) * do_t.astype(jnp.float32), axis=0, keepdims=True
        )
        dq_t = jnp.zeros((HD, width), jnp.float32)
        for d in range(REACH, -1, -1):
            dp = dot(kv[g, d, :, HD:], do_t)
            ds = (scores[d] * inverse * (dp - delta)).astype(jnp.bfloat16)
            dk = dot(ds, q) * scaling
            dv = dot(probs[d], do)
            dq_t = dq_t + dot(kv[g, d, :, :HD].T, ds)
            if d:
                gout[g, d - 1, :, :HD] = dk.astype(jnp.bfloat16)
                gout[g, d - 1, :, HD:] = dv.astype(jnp.bfloat16)

                @pl.when(pos >= d)
                def _():
                    g_copy(g, d).start()

            else:
                own_grads.append((dk, dv))
        att = att_t.T.astype(jnp.bfloat16)
        dq = (dq_t * scaling).T.astype(jnp.bfloat16)
        for j, h in enumerate(heads):
            att_ref[:, h * HD : (h + 1) * HD] = att[j * rows : (j + 1) * rows]
            dq_ref[:, h * HD : (h + 1) * HD] = dq[j * rows : (j + 1) * rows]

    for g in range(kv_heads):
        dk, dv = own_grads[g]
        for d in range(REACH, 0, -1):

            @pl.when(pos + d < n)
            def _():
                g_copy(g, d).wait_recv()

            dk = dk + gin[g, d - 1, :, :HD].astype(jnp.float32)
            dv = dv + gin[g, d - 1, :, HD:].astype(jnp.float32)
        dk_ref[:, g * HD : (g + 1) * HD] = dk.astype(jnp.bfloat16)
        dv_ref[:, g * HD : (g + 1) * HD] = dv.astype(jnp.bfloat16)
    for g in range(kv_heads):
        for d in range(1, REACH + 1):

            @pl.when(pos + d < n)
            def _():
                kv_copy(g, d).wait_send()

            @pl.when(pos >= d)
            def _():
                g_copy(g, d).wait_send()


def per_device(n, reps, queries, key_states, value_states, out_grad, doc_lengths):
    rows, key_width = key_states.shape
    kv_heads = key_width // HD
    width = rows * (queries.shape[1] // key_width)
    vmem = pl.BlockSpec(memory_space=pltpu.VMEM)
    like = [jax.ShapeDtypeStruct(x.shape, x.dtype) for x in (queries, queries, key_states, key_states)]
    sems = pltpu.SemaphoreType.DMA((kv_heads, REACH))
    return tuple(
        pl.pallas_call(
            functools.partial(kernel, n, reps),
            out_shape=like,
            in_specs=[pl.BlockSpec(memory_space=pltpu.SMEM)] + [vmem] * 4,
            out_specs=[vmem] * 4,
            scratch_shapes=[
                pltpu.VMEM((kv_heads, REACH + 1, rows, 2 * HD), jnp.bfloat16),
                pltpu.VMEM((kv_heads, REACH, rows, 2 * HD), jnp.bfloat16),
                pltpu.VMEM((kv_heads, REACH, rows, 2 * HD), jnp.bfloat16),
                pltpu.VMEM((REACH + 1, rows, width), jnp.float32),
                pltpu.VMEM((REACH + 1, rows, width), jnp.bfloat16),
                sems, sems, sems, sems,
            ],
            compiler_params=pltpu.CompilerParams(
                collective_id=0, has_side_effects=True, vmem_limit_bytes=40 * 1024 * 1024
            ),
        )(doc_lengths, queries, key_states, value_states, out_grad)
    )


def solution(mesh):
    split = P(("ctx", "rep"), "tp")
    reps = mesh.shape["rep"]
    return jax.shard_map(
        functools.partial(per_device, mesh.shape["ctx"] * reps, reps),
        mesh=mesh,
        in_specs=(split, split, split, split, P()),
        out_specs=(split, split, split, split),
        check_vma=False,
    )
```

time: 70.2 us -> 34 us (0.48)
  the two profiles are of different devices: /device:TPU:0 before, /device:TPU:27 now
where the time goes in v1:
time: 34 us; the launch traced here: 33.8 us
  Pallas kernels  25.9 us (76%)
  local copies, waits for them, and re-layouts  7.2 us (21%)
  between operations  0.65 us (2%)
    pallas_call x1, Pallas kernels, per_device(): pl.pallas_call(functools.partial(kernel, n, reps), out_shape=like, in_spe...  25.9 us
    unnamed x14, local copies, waits for them, and re-layouts  7.2 us

profile of v1, /device:TPU:27, one launch (start us, length us, event | category | flops | bytes accessed | tf_op | source)
XLA Modules:
  0.0 33.8 jit_solution(3280688144799636234)
XLA Ops:
  0.6 0.0 copy-start
  0.6 1.0 %copy-done = bf16[192,1024]{1,0:T(8,128)(2,1)S(1)} copy-done((bf16[192,1024]{1,0:T(8,128)(2,1)S(1)}, bf16[192,1024]{1,0:T(8,128)(2,1)}, u32[]{:S(2)}) %copy-start) | copy-done | bytes 393240
  1.6 0.0 copy-start.1
  1.6 1.0 %copy-done.1 = bf16[192,1024]{1,0:T(8,128)(2,1)S(1)} copy-done((bf16[192,1024]{1,0:T(8,128)(2,1)S(1)}, bf16[192,1024]{1,0:T(8,128)(2,1)}, u32[]{:S(2)}) %copy-start.1) | copy-done | bytes 393240
  2.6 0.0 copy-start.2
  2.6 0.9 %copy-done.2 = bf16[192,256]{1,0:T(8,128)(2,1)S(1)} copy-done((bf16[192,256]{1,0:T(8,128)(2,1)S(1)}, bf16[192,256]{1,0:T(8,128)(2,1)}, u32[]{:S(2)}) %copy-start.2) | copy-done | bytes 98328
  3.5 0.0 copy-start.3
  3.5 0.9 %copy-done.3 = bf16[192,256]{1,0:T(8,128)(2,1)S(1)} copy-done((bf16[192,256]{1,0:T(8,128)(2,1)S(1)}, bf16[192,256]{1,0:T(8,128)(2,1)}, u32[]{:S(2)}) %copy-start.3) | copy-done | bytes 98328
  4.4 0.0 copy-start.4
  4.4 0.7 %copy-done.4 = s32[7]{0:T(128)S(1)} copy-done((s32[7]{0:T(128)S(1)}, s32[7]{0:T(128)}, u32[]{:S(2)}) %copy-start.4) | copy-done | bytes 52
  5.1 25.9 %shard_map.84 = (bf16[192,1024]{1,0:T(8,128)(2,1)S(1)}, bf16[192,1024]{1,0:T(8,128)(2,1)S(1)}, bf16[192,256]{1,0:T(8,128)(2,1)S(1)}, bf16[192,256]{1,0:T(8,128)(2,1)S(1)}) custom-call(s32[7]{0:T(128)S(1)} %copy-done.4, bf16[192,1024]{1,0:T(8,128)(2,1)S(1)} %copy-done, bf16[192,256]{1,0:T(8,128)(2,1)S(1)} %copy-done.2, bf16[192,256]{1,0:T(8,128)(2,1)S(1)} %copy-done.3, ...), custom_call_target="tpu_custom_call" | custom-call | tf_op jit(solution)/shard_map/pallas_call | solution.py:183
  31.0 0.7 %copy.13 = bf16[192,1024]{1,0:T(8,128)(2,1)} copy(bf16[192,1024]{1,0:T(8,128)(2,1)S(1)} %get-tuple-element.8) | data formatting | bytes 786432
  31.7 0.7 %copy.14 = bf16[192,1024]{1,0:T(8,128)(2,1)} copy(bf16[192,1024]{1,0:T(8,128)(2,1)S(1)} %get-tuple-element.9) | data formatting | bytes 786432
  32.5 0.6 %copy.15 = bf16[192,256]{1,0:T(8,128)(2,1)} copy(bf16[192,256]{1,0:T(8,128)(2,1)S(1)} %get-tuple-element.10) | data formatting | bytes 196608
  33.1 0.6 %copy.16 = bf16[192,256]{1,0:T(8,128)(2,1)} copy(bf16[192,256]{1,0:T(8,128)(2,1)S(1)} %get-tuple-element.11) | data formatting | bytes 196608
Async XLA Ops:
  0.6 1.0 %copy-start = (bf16[192,1024]{1,0:T(8,128)(2,1)S(1)}, bf16[192,1024]{1,0:T(8,128)(2,1)}, u32[]{:S(2)}) copy-start(bf16[192,1024]{1,0:T(8,128)(2,1)} %q_ref.1) | copy-start | bytes 1179652
  1.6 1.0 %copy-start.1 = (bf16[192,1024]{1,0:T(8,128)(2,1)S(1)}, bf16[192,1024]{1,0:T(8,128)(2,1)}, u32[]{:S(2)}) copy-start(bf16[192,1024]{1,0:T(8,128)(2,1)} %do_ref.1) | copy-start | bytes 1179652
  2.6 0.9 %copy-start.2 = (bf16[192,256]{1,0:T(8,128)(2,1)S(1)}, bf16[192,256]{1,0:T(8,128)(2,1)}, u32[]{:S(2)}) copy-start(bf16[192,256]{1,0:T(8,128)(2,1)} %k_ref.1) | copy-start | bytes 294916
  3.5 0.9 %copy-start.3 = (bf16[192,256]{1,0:T(8,128)(2,1)S(1)}, bf16[192,256]{1,0:T(8,128)(2,1)}, u32[]{:S(2)}) copy-start(bf16[192,256]{1,0:T(8,128)(2,1)} %v_ref.1) | copy-start | bytes 294916
  4.4 0.7 %copy-start.4 = (s32[7]{0:T(128)S(1)}, s32[7]{0:T(128)}, u32[]{:S(2)}) copy-start(s32[7]{0:T(128)} %doc_ref.1) | copy-start | bytes 88

commit v2 on v1

--- a/solution.py
+++ b/solution.py
@@ -19,8 +19,8 @@
 
 
 def kernel(
-    n, reps, doc_ref, q_ref, k_ref, v_ref, do_ref, att_ref, dq_ref, dk_ref, dv_ref,
-    kv, gout, gin, scores, probs, kv_send, kv_recv, g_send, g_recv,
+    n, reps, doc_hbm, q_hbm, k_ref, v_ref, do_hbm, att_hbm, dq_hbm, dk_hbm, dv_hbm,
+    att_ref, dq_ref, dk_ref, dv_ref, store, doc_ref, q_ref, do_ref, kv, gout, gin, scores, probs, load, kv_send, kv_recv, g_send, g_recv,
 ):
     rows = q_ref.shape[0]
     kv_heads = k_ref.shape[1] // HD
@@ -41,10 +41,24 @@
             def _():
                 pl.semaphore_signal(barrier, inc=1, device_id=place(peer), device_id_type=MESH)
 
-    for g in range(kv_heads):
-        cols = slice(g * HD, (g + 1) * HD)
-        kv[g, 0, :, :HD] = k_ref[:, cols]
-        kv[g, 0, :, HD:] = v_ref[:, cols]
+    kv_loads = []
+    for g in range(kv_heads):
+        cols = pl.ds(g * HD, HD)
+        for i, ref in enumerate((k_ref, v_ref)):
+            kv_loads.append(
+                pltpu.make_async_copy(
+                    ref.at[:, cols], kv.at[g, 0, :, pl.ds(i * HD, HD)], load.at[3 + 2 * g + i]
+                )
+            )
+    loads = [
+        pltpu.make_async_copy(doc_hbm, doc_ref, load.at[0]),
+        pltpu.make_async_copy(q_hbm, q_ref, load.at[1]),
+        pltpu.make_async_copy(do_hbm, do_ref, load.at[2]),
+    ]
+    for copy in kv_loads + loads:
+        copy.start()
+    for copy in kv_loads:
+        copy.wait()
     pl.semaphore_wait(barrier, jnp.minimum(pos, REACH) + jnp.minimum(n - 1 - pos, REACH))
 
     def kv_copy(g, d):
@@ -78,6 +92,8 @@
             for g in range(kv_heads):
                 gin[g, d - 1] = jnp.zeros(gin.shape[2:], gin.dtype)
 
+    for copy in loads:
+        copy.wait()
     first = pos * rows
     query_pos = first + lax.rem(lax.broadcasted_iota(jnp.int32, (1, width), 1), rows)
     begin = jnp.zeros((1, width), jnp.int32)
@@ -85,6 +101,14 @@
     for i in range(doc_ref.shape[0]):
         end = end + doc_ref[i]
         begin = jnp.maximum(begin, jnp.where(query_pos >= end, end, 0))
+
+    stores = []
+
+    def store_columns(g, i, buf, out):
+        cols = pl.ds(g * (buf.shape[1] // kv_heads), buf.shape[1] // kv_heads)
+        copy = pltpu.make_async_copy(buf.at[:, cols], out.at[:, cols], store.at[g, i])
+        copy.start()
+        stores.append(copy)
 
     own_grads = []
     for g in range(kv_heads):
@@ -147,6 +171,8 @@
         for j, h in enumerate(heads):
             att_ref[:, h * HD : (h + 1) * HD] = att[j * rows : (j + 1) * rows]
             dq_ref[:, h * HD : (h + 1) * HD] = dq[j * rows : (j + 1) * rows]
+        store_columns(g, 0, att_ref, att_hbm)
+        store_columns(g, 1, dq_ref, dq_hbm)
 
     for g in range(kv_heads):
         dk, dv = own_grads[g]
@@ -160,6 +186,10 @@
             dv = dv + gin[g, d - 1, :, HD:].astype(jnp.float32)
         dk_ref[:, g * HD : (g + 1) * HD] = dk.astype(jnp.bfloat16)
         dv_ref[:, g * HD : (g + 1) * HD] = dv.astype(jnp.bfloat16)
+        store_columns(g, 2, dk_ref, dk_hbm)
+        store_columns(g, 3, dv_ref, dv_hbm)
+    for copy in stores:
+        copy.wait()
     for g in range(kv_heads):
         for d in range(1, REACH + 1):
 
@@ -170,33 +200,57 @@
             @pl.when(pos >= d)
             def _():
                 g_copy(g, d).wait_send()
+
+
+def flush(*refs):
+    count = len(refs) // 2
+    copies = [
+        pltpu.make_async_copy(refs[i], refs[count + i], refs[-1].at[i]) for i in range(count)
+    ]
+    for copy in copies:
+        copy.start()
+    for copy in copies:
+        copy.wait()
 
 
 def per_device(n, reps, queries, key_states, value_states, out_grad, doc_lengths):
     rows, key_width = key_states.shape
     kv_heads = key_width // HD
     width = rows * (queries.shape[1] // key_width)
-    vmem = pl.BlockSpec(memory_space=pltpu.VMEM)
     like = [jax.ShapeDtypeStruct(x.shape, x.dtype) for x in (queries, queries, key_states, key_states)]
     sems = pltpu.SemaphoreType.DMA((kv_heads, REACH))
+    hbm = pl.BlockSpec(memory_space=pltpu.HBM)
+    results = pl.pallas_call(
+        functools.partial(kernel, n, reps),
+        out_shape=like,
+        in_specs=[hbm] * 5,
+        out_specs=[hbm] * 4,
+        scratch_shapes=[
+            *(pltpu.VMEM(x.shape, x.dtype) for x in like),
+            pltpu.SemaphoreType.DMA((kv_heads, 4)),
+            pltpu.SMEM(doc_lengths.shape, jnp.int32),
+            pltpu.VMEM(queries.shape, queries.dtype),
+            pltpu.VMEM(out_grad.shape, out_grad.dtype),
+            pltpu.VMEM((kv_heads, REACH + 1, rows, 2 * HD), jnp.bfloat16),
+            pltpu.VMEM((kv_heads, REACH, rows, 2 * HD), jnp.bfloat16),
+            pltpu.VMEM((kv_heads, REACH, rows, 2 * HD), jnp.bfloat16),
+            pltpu.VMEM((REACH + 1, rows, width), jnp.float32),
+            pltpu.VMEM((REACH + 1, rows, width), jnp.bfloat16),
+            pltpu.SemaphoreType.DMA((3 + 2 * kv_heads,)),
+            sems, sems, sems, sems,
+        ],
+        compiler_params=pltpu.CompilerParams(
+            collective_id=0, has_side_effects=True, vmem_limit_bytes=63 * 1024 * 1024
+        ),
+    )(doc_lengths, queries, key_states, value_states, out_grad)
     return tuple(
         pl.pallas_call(
-            functools.partial(kernel, n, reps),
+            flush,
             out_shape=like,
-            in_specs=[pl.BlockSpec(memory_space=pltpu.SMEM)] + [vmem] * 4,
-            out_specs=[vmem] * 4,
-            scratch_shapes=[
-                pltpu.VMEM((kv_heads, REACH + 1, rows, 2 * HD), jnp.bfloat16),
-                pltpu.VMEM((kv_heads, REACH, rows, 2 * HD), jnp.bfloat16),
-                pltpu.VMEM((kv_heads, REACH, rows, 2 * HD), jnp.bfloat16),
-                pltpu.VMEM((REACH + 1, rows, width), jnp.float32),
-                pltpu.VMEM((REACH + 1, rows, width), jnp.bfloat16),
-                sems, sems, sems, sems,
-            ],
-            compiler_params=pltpu.CompilerParams(
-                collective_id=0, has_side_effects=True, vmem_limit_bytes=40 * 1024 * 1024
-            ),
-        )(doc_lengths, queries, key_states, value_states, out_grad)
+            in_specs=[hbm] * 4,
+            out_specs=[hbm] * 4,
+            scratch_shapes=[pltpu.SemaphoreType.DMA((4,))],
+        )(*results)
     )
 
 

time: 34 us -> 57.9 us (1.70)
  Pallas kernels: 25.9 us -> 57.1 us
  local copies, waits for them, and re-layouts: 7.2 us -> 0 us
    pallas_call x0 -> x1, Pallas kernels: none -> 30.9 us  [per_device(): pl.pallas_call(flush, out_shape=like, in_specs=[hbm] * 4, out_specs=[hbm]...]
    unnamed x14 -> x0, local copies, waits for them, and re-layouts: 7.2 us -> none
where the time goes in v2:
time: 57.9 us; the launch traced here: 57.7 us
  Pallas kernels  57.1 us (99%)
  between operations  0.64 us (1%)
    pallas_call x1, Pallas kernels, per_device(): pl.pallas_call(flush, out_shape=like, in_specs=[hbm] * 4, out_specs=[hbm]...  30.9 us
    pallas_call x1, Pallas kernels, per_device(): pl.pallas_call(functools.partial(kernel, n, reps), out_shape=like, in_spe...  26.2 us

profile of v2, /device:TPU:27, one launch (start us, length us, event | category | flops | bytes accessed | tf_op | source)
XLA Modules:
  0.0 57.7 jit_solution(704001920799605389)
XLA Ops:
  0.6 26.2 %shard_map.84 = (bf16[192,1024]{1,0:T(8,128)(2,1)}, bf16[192,1024]{1,0:T(8,128)(2,1)}, bf16[192,256]{1,0:T(8,128)(2,1)}, bf16[192,256]{1,0:T(8,128)(2,1)}) custom-call(s32[7]{0:T(128)} %doc_hbm.1, bf16[192,1024]{1,0:T(8,128)(2,1)} %q_hbm.1, bf16[192,256]{1,0:T(8,128)(2,1)} %k_ref.1, bf16[192,256]{1,0:T(8,128)(2,1)} %v_ref.1, bf16[192,1024]{1,0:T(8,128)(2,1)} %do_hbm.1), custom_call_target="tpu_custom_call" | custom-call | tf_op jit(solution)/shard_map/pallas_call | solution.py:223
  26.8 30.9 %shard_map.85 = (bf16[192,1024]{1,0:T(8,128)(2,1)}, bf16[192,1024]{1,0:T(8,128)(2,1)}, bf16[192,256]{1,0:T(8,128)(2,1)}, bf16[192,256]{1,0:T(8,128)(2,1)}) custom-call(bf16[192,1024]{1,0:T(8,128)(2,1)} %get-tuple-element.8.refs_0_, bf16[192,1024]{1,0:T(8,128)(2,1)} %get-tuple-element.9.refs_1_, bf16[192,256]{1,0:T(8,128)(2,1)} %get-tuple-element.10.refs_2_, ...), custom_call_target="tpu_custom_call" | custom-call | tf_op jit(solution)/shard_map/pallas_call | solution.py:247

commit v3 on v2

--- a/solution.py
+++ b/solution.py
@@ -203,13 +203,16 @@
 
 
 def flush(*refs):
-    count = len(refs) // 2
-    copies = [
-        pltpu.make_async_copy(refs[i], refs[count + i], refs[-1].at[i]) for i in range(count)
-    ]
-    for copy in copies:
+    count = 4
+    ins, outs, bufs, sems = refs[:count], refs[count : 2 * count], refs[2 * count : -1], refs[-1]
+    loads = [pltpu.make_async_copy(ins[i], bufs[i], sems.at[0, i]) for i in range(count)]
+    stores = [pltpu.make_async_copy(bufs[i], outs[i], sems.at[1, i]) for i in range(count)]
+    for copy in loads:
         copy.start()
-    for copy in copies:
+    for load, store in zip(loads, stores):
+        load.wait()
+        store.start()
+    for copy in stores:
         copy.wait()
 
 
@@ -249,7 +252,10 @@
             out_shape=like,
             in_specs=[hbm] * 4,
             out_specs=[hbm] * 4,
-            scratch_shapes=[pltpu.SemaphoreType.DMA((4,))],
+            scratch_shapes=[
+                *(pltpu.VMEM(x.shape, x.dtype) for x in like),
+                pltpu.SemaphoreType.DMA((2, 4)),
+            ],
         )(*results)
     )
 

time: 57.9 us -> 29 us (0.50)
  Pallas kernels: 57.1 us -> 28.2 us
    pallas_call x1, Pallas kernels: 30.9 us -> 2 us  [per_device(): pl.pallas_call(flush, out_shape=like, in_specs=[hbm] * 4, out_specs=[hbm]...]
where the time goes in v3:
time: 29 us; the launch traced here: 28.8 us
  Pallas kernels  28.2 us (97%)
  between operations  0.64 us (2%)
    pallas_call x1, Pallas kernels, per_device(): pl.pallas_call(functools.partial(kernel, n, reps), out_shape=like, in_spe...  26.2 us
    pallas_call x1, Pallas kernels, per_device(): pl.pallas_call(flush, out_shape=like, in_specs=[hbm] * 4, out_specs=[hbm]...  2 us

profile of v3, /device:TPU:27, one launch (start us, length us, event | category | flops | bytes accessed | tf_op | source)
XLA Modules:
  0.0 28.8 jit_solution(4358187992645017400)
XLA Ops:
  0.6 26.2 %shard_map.84 = (bf16[192,1024]{1,0:T(8,128)(2,1)}, bf16[192,1024]{1,0:T(8,128)(2,1)}, bf16[192,256]{1,0:T(8,128)(2,1)}, bf16[192,256]{1,0:T(8,128)(2,1)}) custom-call(s32[7]{0:T(128)} %doc_hbm.1, bf16[192,1024]{1,0:T(8,128)(2,1)} %q_hbm.1, bf16[192,256]{1,0:T(8,128)(2,1)} %k_ref.1, bf16[192,256]{1,0:T(8,128)(2,1)} %v_ref.1, bf16[192,1024]{1,0:T(8,128)(2,1)} %do_hbm.1), custom_call_target="tpu_custom_call" | custom-call | tf_op jit(solution)/shard_map/pallas_call | solution.py:226
  26.8 2.0 %shard_map.85 = (bf16[192,1024]{1,0:T(8,128)(2,1)}, bf16[192,1024]{1,0:T(8,128)(2,1)}, bf16[192,256]{1,0:T(8,128)(2,1)}, bf16[192,256]{1,0:T(8,128)(2,1)}) custom-call(bf16[192,1024]{1,0:T(8,128)(2,1)} %get-tuple-element.8.refs_0_, bf16[192,1024]{1,0:T(8,128)(2,1)} %get-tuple-element.9.refs_1_, bf16[192,256]{1,0:T(8,128)(2,1)} %get-tuple-element.10.refs_2_, ...), custom_call_target="tpu_custom_call" | custom-call | tf_op jit(solution)/shard_map/pallas_call | solution.py:250
